TPU v7x, 256 devices: a whole 4x4x8 slice. The times are simulated.
256 devices in a mesh: dom: 32 (over z, y), samp: 8 (over x, core).
Axes of the slice: x: 4, y: 4, z: 8, core: 2. Of those that a mesh axis runs over, the one named last changes fastest.
Arguments:
- residual: float32 [256, 131072], P('samp', 'dom'), may hold values from -60 to 60
- conductance: float32 [256, 131072], P('samp', 'dom'), may hold values from 0.2 to 2
- capacitance: float32 [256, 131072], P('samp', 'dom'), may hold values from 0.2 to 2
- stamps: float32 [2048, 4, 64, 128], P('dom'), may hold values from -0.375 to 0.375
- block_cols: int32 [2048, 4], P('dom'), may hold values from 0 to 191, as said below
- send_blocks: int32 [32, 32, 4], P('dom'), may hold values from 0 to 63
Outputs:
- update: float32 [256, 131072], P('samp', 'dom')
Inputs may be any that keep to these rules, and one draw needn't show every extreme that they name: `block_cols`: entries below 64 name the partition's own block rows; an entry 64 + s * 4 + j names slot j that partition s sends to this partition, s never the partition itself; entry 0 of a row is the row's own block.
All inputs are finite; a program needn't handle non-finite values.
Results may differ from a plain program's by a relative error of at most 0.00005.
Values sent between devices are 32-bit elements; how exact they have to be, the bound alone decides.
A program may use at most 64 MiB of HBM per device.

v0:
```python
import jax
import jax.numpy as jnp
from jax import lax
from jax.sharding import PartitionSpec as P


def spectral_block(rows, columns, order):
    row_ids = jnp.arange(rows, dtype=jnp.int32)
    column_ids = jnp.arange(columns, dtype=jnp.int32)
    offset = row_ids[:, None] - column_ids[None, :]
    parity = (offset % 2).astype(jnp.float32)
    sign = 1.0 - 2.0 * parity
    angle = jnp.pi / order * offset.astype(jnp.float32)
    nonzero = offset != 0
    safe = jnp.where(nonzero, angle, 0.5)
    value = sign * jnp.cos(safe) / jnp.sin(safe) / order
    return jnp.where(nonzero, value, 0.0)


def body(residual, conductance, capacitance, stamps, block_cols, send_blocks):
    samples_here, unknowns_here = residual.shape
    rows_here, per_entry = block_cols.shape
    width = stamps.shape[2]
    slots_here = send_blocks.shape[2]
    domains = lax.axis_size("dom")
    groups = lax.axis_size("samp")
    period = samples_here * groups
    weights = stamps.reshape(rows_here, per_entry * width, 2 * width)
    flat_send = send_blocks.reshape(-1)
    flat_cols = block_cols.reshape(-1)

    def block_product(picked):
        shaped = picked.reshape(samples_here, rows_here, per_entry * width)
        return jnp.einsum(
            "srm,rmo->sro",
            shaped,
            weights,
            precision=lax.Precision.HIGHEST,
            preferred_element_type=jnp.float32,
        )

    def derivative(charge):
        slab = unknowns_here // groups
        shaped = charge.reshape(samples_here, groups, slab)
        matrix = spectral_block(period, period, period)
        result = jnp.dot(
            matrix,
            lax.all_to_all(shaped, "samp", split_axis=1, concat_axis=0, tiled=True)[:, 0, :],
            precision=lax.Precision.HIGHEST,
            preferred_element_type=jnp.float32,
        )
        moved = lax.all_to_all(result[:, None, :], "samp", split_axis=0, concat_axis=1, tiled=True)
        return moved.reshape(samples_here, unknowns_here)

    def apply_jacobian(field):
        blocks = field.reshape(samples_here, rows_here, width)
        outgoing = jnp.take(blocks, flat_send, axis=1).reshape(
            samples_here, domains, slots_here * width
        )
        incoming = lax.all_to_all(outgoing, "dom", split_axis=1, concat_axis=1, tiled=True)
        arrived = incoming.reshape(samples_here, domains * slots_here, width)
        extended = jnp.concatenate([blocks, arrived], axis=1)
        product = block_product(jnp.take(extended, flat_cols, axis=1))
        direct = product[:, :, :width].reshape(samples_here, unknowns_here)
        charge = product[:, :, width:].reshape(samples_here, unknowns_here) + capacitance * field
        return direct + conductance * field + derivative(charge)

    scale_norm = jnp.sqrt(lax.psum(jnp.sum(residual * residual), ("dom", "samp")))
    basis_one = residual / scale_norm
    image = apply_jacobian(basis_one)
    upper_one = lax.psum(jnp.sum(basis_one * image), ("dom", "samp"))
    image = image - upper_one * basis_one
    lower_one = jnp.sqrt(lax.psum(jnp.sum(image * image), ("dom", "samp")))
    basis_two = image / lower_one
    image = apply_jacobian(basis_two)
    upper_two = lax.psum(jnp.sum(basis_one * image), ("dom", "samp"))
    image = image - upper_two * basis_one
    middle_two = lax.psum(jnp.sum(basis_two * image), ("dom", "samp"))
    image = image - middle_two * basis_two
    lower_two = jnp.sqrt(lax.psum(jnp.sum(image * image), ("dom", "samp")))
    gram_first = upper_one * upper_one + lower_one * lower_one
    gram_cross = upper_one * upper_two + lower_one * middle_two
    gram_second = upper_two * upper_two + middle_two * middle_two + lower_two * lower_two
    target_first = scale_norm * upper_one
    target_second = scale_norm * upper_two
    determinant = gram_first * gram_second - gram_cross * gram_cross
    weight_first = (gram_second * target_first - gram_cross * target_second) / determinant
    weight_second = (gram_first * target_second - gram_cross * target_first) / determinant
    return weight_first * basis_one + weight_second * basis_two


def solution(mesh):
    in_specs = (
        P("samp", "dom"),
        P("samp", "dom"),
        P("samp", "dom"),
        P("dom", None, None, None),
        P("dom", None),
        P("dom", None, None),
    )
    out_specs = P("samp", "dom")
    return jax.shard_map(body, mesh=mesh, in_specs=in_specs, out_specs=out_specs, check_vma=False)
```

profile of v0, /device:TPU:1, one launch (start us, length us, event | category | flops | bytes accessed | tf_op | source)
XLA Modules:
  0.0 688.6 jit_solution(3943485454325701389)
XLA Ops:
  0.0 1.8 multiply_reduce_fusion.5
  2.7 81.4 %psum.42 = f32[]{:T(128)} all-reduce(f32[]{:T(128)} %multiply_reduce_fusion.5), channel_id=1, replica_groups=mesh['dom'=32,'samp'=8] {'dom','samp'}, use_global_device_ids=true, to_apply=%region_1.0 | all-reduce | flops 1 | bytes 8 | tf_op jit(solution)/shard_map/psum | solution.py:68
  89.2 1.5 reshape.73
  90.7 2.9 copy.54
  93.6 5.5 all-to-all-start
  99.4 25.9 %all-to-all-done = f32[32,32,256]{2,0,1:T(8,128)S(1)} async-done(((f32[32,32,256]{2,0,1:T(8,128)}), f32[32,32,256]{2,0,1:T(8,128)S(1)}, u32[]{:S(2)}, u32[]{:S(2)}) %all-to-all-start) | async-done | bytes 1048608 | tf_op jit(solution)/shard_map/all_to_all | solution.py:60
  125.3 1.6 copy.55
  126.9 1.5 reshape.74
  129.7 2.1 pad_maximum_fusion
  131.8 4.6 gather_fusion.1
  136.4 2.7 select_bitcast_fusion.1
  139.1 4.4 copy.58
  143.5 3.5 reshape.76
  147.0 8.1 %fusion.4 = f32[32,64,128]{2,0,1:T(8,128)S(1)} fusion(f32[64,256,128]{2,1,0:T(8,128)} %bitcast.51, f32[32,64,256]{2,1,0:T(8,128)S(1)} %reshape.76), kind=kOutput, calls=%fused_computation.14 | convolution fusion | flops 805306368 | bytes 11534336 | tf_op jit(solution)/shard_map/srm,rmo->sro/dot_general | solution.py:34
  157.6 14.8 %all_to_all.70 = f32[32,8,512]{2,0,1:T(8,128)S(1)} all-to-all(f32[32,8,512]{2,0,1:T(8,128)S(1)} %bitcast.55), channel_id=1, replica_groups=mesh['dom'=32,'samp'=8] {'samp'}, dimensions={1} | all-to-all | bytes 1048576 | tf_op jit(solution)/shard_map/all_to_all | solution.py:48
  172.4 1.7 convolution_bitcast_fusion.1
  174.2 1.3 copy.63
  175.5 5.1 all-to-all-start.2
  181.5 8.6 %all-to-all-done.2 = f32[256,1,512]{2,1,0:T(1,128)} async-done(((f32[256,1,512]{2,1,0:T(1,128)}), f32[256,1,512]{2,1,0:T(1,128)}, u32[]{:S(2)}, u32[]{:S(2)}) %all-to-all-start.2) | async-done | bytes 524320 | tf_op jit(solution)/shard_map/all_to_all | solution.py:52
  190.2 1.3 copy.64
  191.8 1.8 multiply_reduce_fusion.4
  193.6 74.3 %psum.43 = f32[]{:T(128)} all-reduce(f32[]{:T(128)} %get-tuple-element.9), channel_id=1, replica_groups=mesh['dom'=32,'samp'=8] {'dom','samp'}, use_global_device_ids=true, to_apply=%region_3.6 | all-reduce | flops 1 | bytes 8 | tf_op jit(solution)/shard_map/psum | solution.py:71
  267.9 1.4 multiply_reduce_fusion.3
  269.4 73.9 %psum.44 = f32[]{:T(128)} all-reduce(f32[]{:T(128)} %multiply_reduce_fusion.3), channel_id=1, replica_groups=mesh['dom'=32,'samp'=8] {'dom','samp'}, use_global_device_ids=true, to_apply=%region_5.8 | all-reduce | flops 1 | bytes 8 | tf_op jit(solution)/shard_map/psum | solution.py:73
  345.8 2.1 gather_fusion.2
  347.9 1.8 select_bitcast_fusion.2
  349.7 2.6 copy.66
  352.3 2.0 reshape.83
  354.9 31.9 %all_to_all.71 = f32[32,32,256]{2,0,1:T(8,128)S(1)} all-to-all(f32[32,32,256]{2,0,1:T(8,128)S(1)} %copy.67), channel_id=1, replica_groups=mesh['dom'=32,'samp'=8] {'dom'}, dimensions={1} | all-to-all | bytes 2097152 | tf_op jit(solution)/shard_map/all_to_all | solution.py:60
  387.4 1.7 reshape.84
  389.1 2.8 copy.70
  391.9 2.1 pad_maximum_fusion.1
  394.0 4.6 gather_fusion.3
  398.6 2.7 select_bitcast_fusion
  401.3 4.4 copy.71
  405.7 3.5 reshape.85
  409.1 8.1 %fusion.7 = f32[32,64,128]{2,0,1:T(8,128)S(1)} fusion(f32[64,256,128]{2,1,0:T(8,128)} %bitcast.52, f32[32,64,256]{2,1,0:T(8,128)S(1)} %reshape.85), kind=kOutput, calls=%fused_computation.15 | convolution fusion | flops 805306368 | bytes 11534336 | tf_op jit(solution)/shard_map/srm,rmo->sro/dot_general | solution.py:34
  420.7 14.8 %all_to_all.72 = f32[32,8,512]{2,0,1:T(8,128)S(1)} all-to-all(f32[32,8,512]{2,0,1:T(8,128)S(1)} %bitcast.57), channel_id=1, replica_groups=mesh['dom'=32,'samp'=8] {'samp'}, dimensions={1} | all-to-all | bytes 1048576 | tf_op jit(solution)/shard_map/all_to_all | solution.py:48
  435.5 1.7 convolution_bitcast_fusion
  438.6 5.1 all-to-all-start.5
  446.7 6.6 all-to-all-done.5
  453.2 1.3 copy.77
  454.9 1.8 multiply_reduce_fusion.2
  456.7 74.3 %psum.45 = f32[]{:T(128)} all-reduce(f32[]{:T(128)} %get-tuple-element.6), channel_id=1, replica_groups=mesh['dom'=32,'samp'=8] {'dom','samp'}, use_global_device_ids=true, to_apply=%region_7.10 | all-reduce | flops 1 | bytes 8 | tf_op jit(solution)/shard_map/psum | solution.py:76
  532.3 1.4 multiply_reduce_fusion.1
  534.4 73.9 %psum.46 = f32[]{:T(128)} all-reduce(f32[]{:T(128)} %multiply_reduce_fusion.1), channel_id=1, replica_groups=mesh['dom'=32,'samp'=8] {'dom','samp'}, use_global_device_ids=true, to_apply=%region_9.12 | all-reduce | flops 1 | bytes 8 | tf_op jit(solution)/shard_map/psum | solution.py:78
  608.9 2.0 multiply_reduce_fusion
  613.3 73.5 %psum.47 = f32[]{:T(128)} all-reduce(f32[]{:T(128)} %multiply_reduce_fusion), channel_id=1, replica_groups=mesh['dom'=32,'samp'=8] {'dom','samp'}, use_global_device_ids=true, to_apply=%region_11.14 | all-reduce | flops 1 | bytes 8 | tf_op jit(solution)/shard_map/psum | solution.py:80
  (44 shorter events, 20.4 us)
Async XLA Ops:
  89.2 10.0 %copy-start.1 = (s32[64,4]{0,1:T(4,128)S(1)}, s32[64,4]{0,1:T(4,128)}, u32[]{:S(2)}) copy-start(s32[64,4]{0,1:T(4,128)} %param.14) | copy-start | bytes 3076
  93.6 31.8 %all-to-all-start = ((f32[32,32,256]{2,0,1:T(8,128)}), f32[32,32,256]{2,0,1:T(8,128)S(1)}, u32[]{:S(2)}, u32[]{:S(2)}) async-start(f32[32,32,256]{2,0,1:T(8,128)} %copy.54), calls=%async_computation | async-start | bytes 2097152 | tf_op jit(solution)/shard_map/all_to_all | solution.py:60
  155.1 1.4 copy-start
  175.5 14.7 %all-to-all-start.2 = ((f32[256,1,512]{2,1,0:T(1,128)}), f32[256,1,512]{2,1,0:T(1,128)}, u32[]{:S(2)}, u32[]{:S(2)}) async-start(f32[256,1,512]{2,1,0:T(1,128)} %copy.63), calls=%async_computation.2 | async-start | bytes 1048576 | tf_op jit(solution)/shard_map/all_to_all | solution.py:52
  438.6 14.7 %all-to-all-start.5 = ((f32[256,1,512]{2,1,0:T(1,128)}), f32[256,1,512]{2,1,0:T(1,128)}, u32[]{:S(2)}, u32[]{:S(2)}) async-start(f32[256,1,512]{2,1,0:T(1,128)} %copy.76), calls=%async_computation.5 | async-start | bytes 1048576 | tf_op jit(solution)/shard_map/all_to_all | solution.py:52
where the time goes:
time: 695 us; the launch traced here: 689 us
  blocking collectives  513 us (74%)
  local copies, waits for them, and re-layouts  62.7 us (9%)
  waiting for transfers between devices  41.1 us (6%)
  other arithmetic  27 us (4%)
  matrix products  19.7 us (3%)
  starting transfers between devices  15.7 us (2%)
  between operations  9.76 us (1%)
    psum x1, blocking collectives, body(): lax.psum(jnp.sum(residual * residual), ('dom', 'samp'))  81.4 us
    psum x1, blocking collectives, body(): upper_one = lax.psum(jnp.sum(basis_one * image), ('dom', 'samp'))  74.3 us
    psum x1, blocking collectives, body(): upper_two = lax.psum(jnp.sum(basis_one * image), ('dom', 'samp'))  74.3 us
    psum x1, blocking collectives, body(): middle_two = lax.psum(jnp.sum(basis_two * image), ('dom', 'samp'))  73.9 us
    psum x1, blocking collectives, body(): lower_one = jnp.sqrt(lax.psum(jnp.sum(image * image), ('dom', 'samp')))  73.9 us
    psum x1, blocking collectives, body(): lower_two = jnp.sqrt(lax.psum(jnp.sum(image * image), ('dom', 'samp')))  73.5 us
    all_to_all x1, blocking collectives, apply_jacobian(): lax.all_to_all(outgoing, 'dom', split_axis=1, concat_axis=1, tiled=True)  31.9 us
    all_to_all x2, blocking collectives, derivative(): lax.all_to_all(shaped, 'samp', split_axis=1, concat_axis=0, tiled=True)  29.6 us
  transfers between devices with their start and end apart: 3, of which 3 were waited for; matrix products, arithmetic and copies ran while one was open for 0% of the time, Pallas kernels for 0%

commit v1 on v0

v1 whole, which is shorter than its diff:
```python
import jax
import jax.numpy as jnp
import ml_dtypes
import numpy as np
from jax import lax
from jax.experimental import pallas as pl
from jax.experimental.pallas import tpu as pltpu
from jax.sharding import PartitionSpec as P

MESH = pl.DeviceIdType.MESH
F32 = jnp.float32
BF16 = jnp.bfloat16

DOM = 32
SAMP = 8
ROWS = 64
SLOTS = 4
CH = 4
T = 8
N = 4096
SLAB = N // SAMP
ORDER = 256
CHUNK_ROWS = SAMP * T


def derivative_matrix():
    place = np.arange(ORDER)
    chunk, group, inner = place // CHUNK_ROWS, (place // T) % SAMP, place % T
    sample = group * (CH * T) + chunk * T + inner
    offset = sample[:, None] - sample[None, :]
    sign = 1.0 - 2.0 * (offset % 2)
    angle = np.where(offset != 0, np.pi / ORDER * offset, 0.5)
    value = np.where(offset != 0, sign / np.tan(angle) / ORDER, 0.0)
    high = value.astype(np.float32).astype(ml_dtypes.bfloat16)
    low = (value - high.astype(np.float64)).astype(np.float32).astype(ml_dtypes.bfloat16)
    return np.concatenate(
        [high.reshape(CH, CHUNK_ROWS, ORDER), low.reshape(CH, CHUNK_ROWS, ORDER)], axis=1
    )


def split(x):
    high = x.astype(BF16)
    return high, (x - high.astype(F32)).astype(BF16)


def kernel(
    cols, send, r_hbm, cond_hbm, cap_hbm, w_hbm, dm_hbm, out,
    field, cond, cap, w32, w16, dm, dup, ext,
    sbuf, rbuf, q, e, bq, be, br, bh, bl, z1b, part, red_s, red_d,
    load_sem, dom_ss, dom_rs, fq_ss, fq_rs, fe_ss, fe_rs, fr_ss, fr_rs, back_ss, back_rs,
    rs_ss, rs_rs, rd_ss, rd_rs,
):
    d = lax.axis_index("dom")
    s = lax.axis_index("samp")
    lanes = lax.broadcasted_iota(jnp.int32, (T, 128), 1)
    left = lanes < 64
    left16 = lax.broadcasted_iota(jnp.int32, (2 * T, 128), 1) < 64

    loads = [
        pltpu.make_async_copy(src, dst, load_sem.at[i])
        for i, (src, dst) in enumerate(
            ((r_hbm, field.at[0]), (cond_hbm, cond), (cap_hbm, cap), (w_hbm, w32), (dm_hbm, dm))
        )
    ]
    for copy in loads:
        copy.start()

    barrier = pltpu.get_barrier_semaphore()

    def greet_dom(k, _):
        pl.semaphore_signal(barrier, inc=1, device_id=(lax.rem(d + k, DOM), s), device_id_type=MESH)
        return 0

    def greet_samp(k, _):
        pl.semaphore_signal(barrier, inc=1, device_id=(d, lax.rem(s + k, SAMP)), device_id_type=MESH)
        return 0

    lax.fori_loop(1, DOM, greet_dom, 0)
    lax.fori_loop(1, SAMP, greet_samp, 0)

    def rows_of(c):
        return pl.ds(pl.multiple_of(c * T, T), T)

    def slab_of(k):
        return pl.ds(pl.multiple_of(k * SLAB, SLAB), SLAB)

    def place_of(c, group):
        return pl.ds(pl.multiple_of((c * SAMP + group) * T, T), T)

    def await_bytes(ref, sem):
        pltpu.make_async_copy(ref, ref, sem).wait()

    def widen(j, c):
        def step(p, _):
            tile = field[j, rows_of(c), pl.ds(pl.multiple_of(p * 128, 128), 128)]
            turned = pltpu.roll(tile, 64, 1)
            dup[2 * p] = jnp.where(left, tile, turned)
            dup[2 * p + 1] = jnp.where(left, turned, tile)
            return 0

        lax.fori_loop(0, ROWS // 2, step, 0, unroll=4)

    def pack(j, c):
        def step(k, _):
            to = lax.rem(d + k, DOM)
            for h in range(2):
                sbuf[j, c, to, h] = jnp.where(
                    left, dup[send[to * SLOTS + 2 * h]], dup[send[to * SLOTS + 2 * h + 1]]
                )
            return 0

        lax.fori_loop(1, DOM, step, 0)

    def send_dom(j, c):
        def step(k, _):
            to = lax.rem(d + k, DOM)
            pltpu.make_async_remote_copy(
                src_ref=sbuf.at[j, c, to], dst_ref=rbuf.at[j, c, d],
                send_sem=dom_ss.at[j], recv_sem=dom_rs.at[j, c],
                device_id=(to, s), device_id_type=MESH,
            ).start()
            return 0

        lax.fori_loop(1, DOM, step, 0)

    def forward(src, dst, c, send_sem, recv_sem):
        def step(k, _):
            to = lax.rem(s + k, SAMP)
            pltpu.make_async_remote_copy(
                src_ref=src.at[rows_of(c), slab_of(to)], dst_ref=dst.at[place_of(c, s)],
                send_sem=send_sem, recv_sem=recv_sem,
                device_id=(d, to), device_id_type=MESH,
            ).start()
            return 0

        lax.fori_loop(1, SAMP, step, 0)
        dst[place_of(c, s), :] = src[rows_of(c), slab_of(s)]

    def spread(tile, at):
        turned = pltpu.roll(tile, 64, 1)
        for i, both in enumerate((jnp.where(left, tile, turned), jnp.where(left, turned, tile))):
            high = both.astype(BF16).astype(F32)
            ext[at + i] = jnp.concatenate([high, both - high], axis=0).astype(BF16)

    def product(j, c):
        def local(p, _):
            spread(field[j, rows_of(c), pl.ds(pl.multiple_of(p * 128, 128), 128)], 2 * p)
            return 0

        lax.fori_loop(0, ROWS // 2, local, 0, unroll=4)
        await_bytes(rbuf.at[j, c, pl.ds(0, DOM - 1)], dom_rs.at[j, c])

        def remote(k, _):
            for h in range(2):
                spread(rbuf[j, c, k, h], ROWS + SLOTS * k + 2 * h)
            return 0

        lax.fori_loop(0, DOM, remote, 0, unroll=2)

        def one_row(row):
            picked = [ext[cols[row * 4 + k]] for k in range(4)]
            lhs = jnp.concatenate(
                [jnp.where(left16, picked[0], picked[1]), jnp.where(left16, picked[2], picked[3])], axis=1
            )
            got = jnp.dot(lhs, w16[row], preferred_element_type=F32)
            return (got[:T, :128] + (got[T:, :128] + got[:T, 128:])) + got[T:, 128:]

        def pair(p, _):
            even, odd = one_row(2 * p), one_row(2 * p + 1)
            at = pl.ds(pl.multiple_of(p * 128, 128), 128)
            value = field[j, rows_of(c), at]
            q[j, rows_of(c), at] = jnp.where(left, pltpu.roll(even, 64, 1), odd) + cap[rows_of(c), at] * value
            e[j, rows_of(c), at] = jnp.where(left, even, pltpu.roll(odd, 64, 1)) + cond[rows_of(c), at] * value
            return 0

        lax.fori_loop(0, ROWS // 2, pair, 0, unroll=4)
        forward(q.at[j], bq.at[j], c, fq_ss.at[j], fq_rs.at[j, c])
        forward(e.at[j], be.at[j], c, fe_ss.at[j], fe_rs.at[j, c])

    def split_charge(j):
        def step(c, _):
            await_bytes(bq.at[j, pl.ds(0, CHUNK_ROWS - T)], fq_rs.at[j, c])
            at = pl.ds(pl.multiple_of(c * CHUNK_ROWS, CHUNK_ROWS), CHUNK_ROWS)
            bh[at, :], bl[at, :] = split(bq[j, at, :])
            return 0

        lax.fori_loop(0, CH, step, 0)

    def slope(c):
        first = jnp.dot(dm[c], bh[...], preferred_element_type=F32)
        second = jnp.dot(dm[c, pl.ds(0, CHUNK_ROWS)], bl[...], preferred_element_type=F32)
        return first[:CHUNK_ROWS] + (first[CHUNK_ROWS:] + second)

    def fold(x):
        x = jnp.sum(x.reshape(-1, T, x.shape[-1]), axis=0)
        return sum(x[:, i * 128 : (i + 1) * 128] for i in range(x.shape[-1] // 128))

    def send_part(i):
        red_s[i, s] = part[i]

        def step(k, _):
            pltpu.make_async_remote_copy(
                src_ref=part.at[i], dst_ref=red_s.at[i, s], send_sem=rs_ss.at[i], recv_sem=rs_rs.at[i],
                device_id=(d, lax.rem(s + k, SAMP)), device_id_type=MESH,
            ).start()
            return 0

        lax.fori_loop(1, SAMP, step, 0)

    def pass_part(i):
        await_bytes(red_s.at[i, pl.ds(0, SAMP - 1)], rs_rs.at[i])
        red_d[i, d] = jnp.sum(red_s[i], axis=0)

        def step(k, _):
            pltpu.make_async_remote_copy(
                src_ref=red_d.at[i, d], dst_ref=red_d.at[i, d], send_sem=rd_ss.at[i], recv_sem=rd_rs.at[i],
                device_id=(lax.rem(d + k, DOM), s), device_id_type=MESH,
            ).start()
            return 0

        lax.fori_loop(1, DOM, step, 0)

    def sums(i):
        await_bytes(red_d.at[i, pl.ds(0, DOM - 1)], rd_rs.at[i])
        total = jnp.sum(red_d[i], axis=0)
        return [jnp.sum(total[k : k + 1, :], axis=1, keepdims=True) for k in range(3)]

    def partial_sums(parts):
        rows = [jnp.sum(x, axis=0, keepdims=True) for x in parts]
        return jnp.concatenate(rows + [jnp.zeros((T - len(rows), 128), F32)], axis=0)

    loads[0].wait()
    for j in range(2):
        for c in range(CH):
            rbuf[j, c, d] = jnp.zeros((2, T, 128), F32)
    widen(0, 0)
    pack(0, 0)
    pl.semaphore_wait(barrier, DOM + SAMP - 2)
    send_dom(0, 0)

    def early(c, _):
        widen(0, c)
        pack(0, c)
        send_dom(0, c)
        return 0

    lax.fori_loop(1, CH, early, 0)

    def share_residual(c, _):
        forward(field.at[0], br, c, fr_ss, fr_rs)
        return 0

    lax.fori_loop(0, CH, share_residual, 0)

    loads[3].wait()

    def halves(row, _):
        high, low = split(w32[row])
        w16[row, :, 0:128] = high
        w16[row, :, 128:256] = low
        return 0

    lax.fori_loop(0, ROWS, halves, 0)
    for i in (1, 2, 4):
        loads[i].wait()

    def first(c, _):
        product(0, c)
        return 0

    lax.fori_loop(0, CH, first, 0)
    split_charge(0)

    def slopes(c, _):
        at = pl.ds(pl.multiple_of(c * CHUNK_ROWS, CHUNK_ROWS), CHUNK_ROWS)
        got = slope(c)
        await_bytes(be.at[0, pl.ds(0, CHUNK_ROWS - T)], fe_rs.at[0, c])
        z1b[at, :] = got + be[0, at, :]

        def step(k, _):
            to = lax.rem(s + k, SAMP)
            pltpu.make_async_remote_copy(
                src_ref=z1b.at[place_of(c, to)], dst_ref=field.at[1, rows_of(c), slab_of(s)],
                send_sem=back_ss, recv_sem=back_rs.at[c],
                device_id=(d, to), device_id_type=MESH,
            ).start()
            return 0

        lax.fori_loop(1, SAMP, step, 0)
        field[1, rows_of(c), slab_of(s)] = z1b[place_of(c, s), :]
        return 0

    lax.fori_loop(0, CH, slopes, 0)

    def again(c, _):
        await_bytes(field.at[1, rows_of(c), pl.ds(0, N - SLAB)], back_rs.at[c])
        widen(1, c)
        pack(1, c)
        send_dom(1, c)
        return 0

    lax.fori_loop(0, CH, again, 0)

    await_bytes(br.at[pl.ds(0, ORDER - ORDER // SAMP)], fr_rs)
    part[0] = partial_sums([fold(br[...] * br[...]), fold(br[...] * z1b[...]), fold(z1b[...] * z1b[...])])
    send_part(0)
    product(1, 0)
    pass_part(0)

    def second(c, _):
        product(1, c)
        return 0

    lax.fori_loop(1, CH, second, 0)
    square, cross, image = sums(0)
    share = cross / square
    split_charge(1)

    def dots(c, carry):
        at = pl.ds(pl.multiple_of(c * CHUNK_ROWS, CHUNK_ROWS), CHUNK_ROWS)
        got = slope(c)
        await_bytes(be.at[1, pl.ds(0, CHUNK_ROWS - T)], fe_rs.at[1, c])
        one = z1b[at, :]
        two = got + be[1, at, :] - share * one
        return tuple(a + b for a, b in zip(carry, (fold(br[at, :] * two), fold(one * two), fold(two * two)), strict=True))

    zero = jnp.zeros((T, 128), F32)
    part[1] = partial_sums(lax.fori_loop(0, CH, dots, (zero, zero, zero)))
    send_part(1)
    pass_part(1)
    target, gram_cross, gram_second = sums(1)
    determinant = image * gram_second - gram_cross * gram_cross
    weight_first = (gram_second * cross - gram_cross * target) / determinant
    weight_second = (image * target - gram_cross * cross) / determinant

    def finish(c, _):
        residual = field[0, rows_of(c), :]
        out[rows_of(c), :] = weight_first * residual + weight_second * (field[1, rows_of(c), :] - share * residual)
        return 0

    lax.fori_loop(0, CH, finish, 0)

    for j in range(2):
        await_bytes(sbuf.at[j, :, pl.ds(0, DOM - 1)], dom_ss.at[j])
        await_bytes(q.at[j, :, pl.ds(0, N - SLAB)], fq_ss.at[j])
        await_bytes(e.at[j, :, pl.ds(0, N - SLAB)], fe_ss.at[j])
        await_bytes(red_s.at[j, pl.ds(0, SAMP - 1)], rs_ss.at[j])
        await_bytes(red_d.at[j, pl.ds(0, DOM - 1)], rd_ss.at[j])
    await_bytes(br.at[pl.ds(0, ORDER - ORDER // SAMP)], fr_ss)
    await_bytes(z1b.at[pl.ds(0, ORDER - ORDER // SAMP)], back_ss)


def body(residual, conductance, capacitance, stamps, block_cols, send_blocks):
    smem = pl.BlockSpec(memory_space=pltpu.SMEM)
    anywhere = pl.BlockSpec(memory_space=pl.ANY)
    dma = pltpu.SemaphoreType.DMA
    here = (CH * T, N)
    all_samples = (ORDER, SLAB)
    vmem = pltpu.VMEM
    return pl.pallas_call(
        kernel,
        out_shape=jax.ShapeDtypeStruct(here, F32),
        in_specs=[smem, smem] + [anywhere] * 5,
        out_specs=pl.BlockSpec(memory_space=pltpu.VMEM),
        scratch_shapes=[
            vmem((2, *here), F32), vmem(here, F32), vmem(here, F32),
            vmem((ROWS, 256, 128), F32), vmem((ROWS, 256, 256), BF16),
            vmem((CH, 2 * CHUNK_ROWS, ORDER), BF16),
            vmem((ROWS, T, 128), F32), vmem((ROWS + SLOTS * DOM, 2 * T, 128), BF16),
            vmem((2, CH, DOM, 2, T, 128), F32), vmem((2, CH, DOM, 2, T, 128), F32),
            vmem((2, *here), F32), vmem((2, *here), F32),
            vmem((2, *all_samples), F32), vmem((2, *all_samples), F32), vmem(all_samples, F32),
            vmem(all_samples, BF16), vmem(all_samples, BF16), vmem(all_samples, F32),
            vmem((2, T, 128), F32), vmem((2, SAMP, T, 128), F32), vmem((2, DOM, T, 128), F32),
            dma((5,)), dma((2,)), dma((2, CH)), dma((2,)), dma((2, CH)), dma((2,)), dma((2, CH)), dma, dma, dma, dma((CH,)),
            dma((2,)), dma((2,)), dma((2,)), dma((2,)),
        ],
        compiler_params=pltpu.CompilerParams(
            collective_id=0, has_side_effects=True, vmem_limit_bytes=56 * 2**20
        ),
        cost_estimate=pl.CostEstimate(flops=1_200_000_000, bytes_accessed=12_000_000, transcendentals=0),
        name="gmres_step",
    )(
        block_cols.reshape(-1), send_blocks.reshape(-1), residual, conductance, capacitance,
        stamps.reshape(ROWS, 256, 128), jnp.asarray(derivative_matrix()),
    )


def solution(mesh):
    in_specs = (
        P("samp", "dom"),
        P("samp", "dom"),
        P("samp", "dom"),
        P("dom", None, None, None),
        P("dom", None),
        P("dom", None, None),
    )
    return jax.shard_map(body, mesh=mesh, in_specs=in_specs, out_specs=P("samp", "dom"), check_vma=False)
```

time: 695 us -> 105 us (0.15)
  blocking collectives: 513 us -> 0 us
  Pallas kernels: 0 us -> 99.9 us
  local copies, waits for them, and re-layouts: 62.7 us -> 4.77 us
  waiting for transfers between devices: 41.1 us -> 0 us
  other arithmetic: 27 us -> 0 us
  matrix products: 19.7 us -> 0 us
  starting transfers between devices: 15.7 us -> 0 us
  between operations: 9.76 us -> 0.01 us
    psum x6 -> x0, blocking collectives: 451 us -> none  [the longest x1 81.4 us: body(): lax.psum(jnp.sum(residual * residual), ('dom', 'samp'))]
    pallas_call x0 -> x1, Pallas kernels: none -> 99.9 us  [body(): pl.pallas_call(kernel, out_shape=jax.ShapeDtypeStruct(here, F32), in_spec...]
    all_to_all x3 -> x0, blocking collectives: 61.5 us -> none  [the longest x1 31.9 us: apply_jacobian(): lax.all_to_all(outgoing, 'dom', split_axis=1, concat_axis=1, tiled=True)]
    all_to_all x3 -> x0, waiting for transfers between devices: 41.1 us -> none  [the longest x1 25.9 us: apply_jacobian(): lax.all_to_all(outgoing, 'dom', split_axis=1, concat_axis=1, tiled=True)]
    reshape x22 -> x2, local copies, waits for them, and re-layouts: 25.7 us -> 1.37 us  [the longest x1 0.7 us: body(): send_blocks.reshape(-1)]
    dot_general x4 -> x0, matrix products: 19.7 us -> none  [the longest x2 16.2 us: block_product(): jnp.einsum('srm,rmo->sro', shaped, weights, precision=lax.Precision.HIGHE...]
    all_to_all x3 -> x0, starting transfers between devices: 15.7 us -> none  [the longest x2 10.1 us: derivative(): lax.all_to_all(result[:, None, :], 'samp', split_axis=0, concat_axis=1, t...]
    select_n x4 -> x0, local copies, waits for them, and re-layouts: 12.5 us -> none  [the longest x2 8.71 us: apply_jacobian(): product = block_product(jnp.take(extended, flat_cols, axis=1))]
  transfers between devices with their start and end apart: 3 -> 0, of which waited for: 3 -> 0; matrix products, arithmetic and copies ran while one was open for 0% -> 0% of each run, Pallas kernels for 0% -> 0%
where the time goes in v1:
time: 105 us
  Pallas kernels  99.9 us (95%)
  local copies, waits for them, and re-layouts  4.77 us (5%)
    pallas_call x1, Pallas kernels, body(): pl.pallas_call(kernel, out_shape=jax.ShapeDtypeStruct(here, F32), in_spec...  99.9 us
    unnamed x3, local copies, waits for them, and re-layouts  3.4 us

profile of v1, /device:TPU:1, one launch (start us, length us, event | category | flops | bytes accessed | tf_op | source)
XLA Modules:
  0.0 104.7 jit_solution(7908118444159847007)
XLA Ops:
  0.0 0.8 copy.10
  0.8 0.7 reshape.10.send
  1.5 0.8 copy.9
  2.2 0.7 reshape.9.cols
  2.9 99.9 %gmres_step.1 = f32[32,4096]{1,0:T(8,128)} custom-call(s32[256]{0:T(256)} %reshape.9.cols, s32[128]{0:T(128)} %reshape.10.send, f32[32,4096]{1,0:T(8,128)} %r_hbm.1, f32[32,4096]{1,0:T(8,128)} %cond_hbm.1, f32[32,4096]{1,0:T(8,128)} %cap_hbm.1, f32[64,256,128]{2,1,0:T(8,128)} %bitcast.1, bf16[4,128,256]{2,1,0:T(8,128)(2,1)} %constant.2.clone.dm_hbm), custom_call_target="tpu_custom_call" | custom-call | flops 1200000000 | bytes 12000000 | tf_op jit(solution)/shard_map/gmres_step/pallas_call | solution.py:360
  102.8 1.9 %copy.12 = f32[32,4096]{1,0:T(8,128)} copy(f32[32,4096]{1,0:T(8,128)} %gmres_step.1) | data formatting | bytes 1048576

commit v2 on v1

v2 whole, which is shorter than its diff:
```python
import jax
import jax.numpy as jnp
import ml_dtypes
import numpy as np
from jax import lax
from jax.experimental import pallas as pl
from jax.experimental.pallas import tpu as pltpu
from jax.sharding import PartitionSpec as P

MESH = pl.DeviceIdType.MESH
F32 = jnp.float32
BF16 = jnp.bfloat16

DOM = 32
SAMP = 8
ROWS = 64
SLOTS = 4
CH = 4
T = 8
N = 4096
SLAB = N // SAMP
ORDER = 256
CHUNK_ROWS = SAMP * T


def derivative_matrix():
    place = np.arange(ORDER)
    chunk, group, inner = place // CHUNK_ROWS, (place // T) % SAMP, place % T
    sample = group * (CH * T) + chunk * T + inner
    offset = sample[:, None] - sample[None, :]
    sign = 1.0 - 2.0 * (offset % 2)
    angle = np.where(offset != 0, np.pi / ORDER * offset, 0.5)
    value = np.where(offset != 0, sign / np.tan(angle) / ORDER, 0.0)
    high = value.astype(np.float32).astype(ml_dtypes.bfloat16)
    low = (value - high.astype(np.float64)).astype(np.float32).astype(ml_dtypes.bfloat16)
    return np.concatenate(
        [high.reshape(CH, CHUNK_ROWS, ORDER), low.reshape(CH, CHUNK_ROWS, ORDER)], axis=1
    )


def split(x):
    high = x.astype(BF16)
    return high, (x - high.astype(F32)).astype(BF16)


def kernel(
    cols, send, r_hbm, cond_hbm, cap_hbm, w_hbm, dm_hbm, out,
    field, cond, cap, w32, w16, dm, dup, ext,
    sbuf, rbuf, q, e, bq, be, br, bh, bl, z1b, slo, back, part, red_s, red_d,
    load_sem, dom_ss, dom_rs, fq_ss, fq_rs, fe_ss, fe_rs, fr_ss, fr_rs, back_ss, back_rs,
    rs_ss, rs_rs, rd_ss, rd_rs,
):
    d = lax.axis_index("dom")
    s = lax.axis_index("samp")
    left = lax.broadcasted_iota(jnp.int32, (T, 128), 1) < 64
    left16 = lax.broadcasted_iota(jnp.int32, (2 * T, 128), 1) < 64

    loads = [
        pltpu.make_async_copy(src, dst, load_sem.at[i])
        for i, (src, dst) in enumerate(
            ((r_hbm, field.at[0]), (w_hbm, w32), (cond_hbm, cond), (cap_hbm, cap), (dm_hbm, dm))
        )
    ]
    for copy in loads:
        copy.start()

    barrier = pltpu.get_barrier_semaphore()

    def over_dom(act):
        act(lax.rem(d + DOM // 2, DOM))

        def step(m, _):
            act(lax.rem(d + DOM // 2 + m, DOM))
            act(lax.rem(d + DOM // 2 - m, DOM))
            return 0

        lax.fori_loop(1, DOM // 2, step, 0)

    def over_samp(act):
        for k in (4, 3, 5, 2, 6, 1, 7):
            act(lax.rem(s + k, SAMP))

    def greet(to_dom, to_samp):
        pl.semaphore_signal(barrier, inc=1, device_id=(to_dom, to_samp), device_id_type=MESH)

    over_dom(lambda to: greet(to, s))
    over_samp(lambda to: greet(d, to))

    def remote(src, dst, send_sem, recv_sem, to):
        pltpu.make_async_remote_copy(
            src_ref=src, dst_ref=dst, send_sem=send_sem, recv_sem=recv_sem, device_id=to, device_id_type=MESH
        ).start()

    def rows_of(c):
        return pl.ds(pl.multiple_of(c * T, T), T)

    def chunk_of(c):
        return pl.ds(pl.multiple_of(c * CHUNK_ROWS, CHUNK_ROWS), CHUNK_ROWS)

    def tile_of(p):
        return pl.ds(pl.multiple_of(p * 128, 128), 128)

    def slab_of(k):
        return pl.ds(pl.multiple_of(k * SLAB, SLAB), SLAB)

    def place_of(c, group):
        return pl.ds(pl.multiple_of((c * SAMP + group) * T, T), T)

    def await_bytes(ref, sem):
        pltpu.make_async_copy(ref, ref, sem).wait()

    def widen(j, c):
        def step(p, _):
            tile = field[j, rows_of(c), tile_of(p)]
            turned = pltpu.roll(tile, 64, 1)
            dup[2 * p] = jnp.where(left, tile, turned)
            dup[2 * p + 1] = jnp.where(left, turned, tile)
            return 0

        lax.fori_loop(0, ROWS // 2, step, 0, unroll=16)

    def pack(j, c, to):
        for h in range(2):
            sbuf[j, c, to, h] = jnp.where(left, dup[send[2 * h, to]], dup[send[2 * h + 1, to]])

    def send_dom(j, c, to):
        remote(sbuf.at[j, c, to], rbuf.at[j, c, d], dom_ss.at[j], dom_rs.at[j, c], (to, s))

    def pack_and_send(j, c):
        def act(to):
            pack(j, c, to)
            send_dom(j, c, to)

        over_dom(act)

    def forward(src, dst, c, send_sem, recv_sem):
        over_samp(
            lambda to: remote(src.at[rows_of(c), slab_of(to)], dst.at[place_of(c, s)], send_sem, recv_sem, (d, to))
        )
        dst[place_of(c, s), :] = src[rows_of(c), slab_of(s)]

    def spread(tile, at):
        turned = pltpu.roll(tile, 64, 1)
        for i, both in enumerate((jnp.where(left, tile, turned), jnp.where(left, turned, tile))):
            high = both.astype(BF16).astype(F32)
            ext[at + i] = jnp.concatenate([high, both - high], axis=0).astype(BF16)

    def product(j, c):
        def local(p, _):
            spread(field[j, rows_of(c), tile_of(p)], 2 * p)
            return 0

        lax.fori_loop(0, ROWS // 2, local, 0, unroll=16)
        await_bytes(rbuf.at[j, c, pl.ds(0, DOM - 1)], dom_rs.at[j, c])

        def arrived(k, _):
            for h in range(2):
                spread(rbuf[j, c, k, h], ROWS + SLOTS * k + 2 * h)
            return 0

        lax.fori_loop(0, DOM, arrived, 0, unroll=8)

        def one_row(row):
            picked = [ext[cols[k, row]] for k in range(4)]
            lhs = jnp.concatenate(
                [jnp.where(left16, picked[0], picked[1]), jnp.where(left16, picked[2], picked[3])], axis=1
            )
            got = jnp.dot(lhs, w16[row], preferred_element_type=F32)
            return (got[:T, :128] + (got[T:, :128] + got[:T, 128:])) + got[T:, 128:]

        def slabs(half, _):
            for start, way in ((4, 2), (3, -2), (5, 2), (2, -2)):
                to = lax.rem(s + start + way * half, SAMP)
                for i in range(SLAB // 128):
                    p = to * (SLAB // 128) + i
                    even, odd = one_row(2 * p), one_row(2 * p + 1)
                    value = field[j, rows_of(c), tile_of(p)]
                    q[j, rows_of(c), tile_of(p)] = (
                        jnp.where(left, pltpu.roll(even, 64, 1), odd) + cap[rows_of(c), tile_of(p)] * value
                    )
                    e[j, rows_of(c), tile_of(p)] = (
                        jnp.where(left, even, pltpu.roll(odd, 64, 1)) + cond[rows_of(c), tile_of(p)] * value
                    )

                @pl.when(to != s)
                def _():
                    remote(
                        q.at[j, rows_of(c), slab_of(to)], bq.at[j, place_of(c, s)], fq_ss.at[j], fq_rs.at[j, c], (d, to)
                    )

            return 0

        lax.fori_loop(0, 2, slabs, 0)
        bq[j, place_of(c, s), :] = q[j, rows_of(c), slab_of(s)]

    def split_charge(j, c):
        await_bytes(bq.at[j, pl.ds(0, CHUNK_ROWS - T)], fq_rs.at[j, c])
        bh[chunk_of(c), :], bl[chunk_of(c), :] = split(bq[j, chunk_of(c), :])

    def slope(c):
        first = jnp.dot(dm[c], bh[...], preferred_element_type=F32)
        second = jnp.dot(dm[c, pl.ds(0, CHUNK_ROWS)], bl[...], preferred_element_type=F32)
        return first[:CHUNK_ROWS] + (first[CHUNK_ROWS:] + second)

    def fold(x):
        x = jnp.sum(x.reshape(-1, T, x.shape[-1]), axis=0)
        return sum(x[:, i * 128 : (i + 1) * 128] for i in range(x.shape[-1] // 128))

    def add_up(parts, terms):
        return tuple(a + fold(b) for a, b in zip(parts, terms, strict=True))

    def send_part(i, parts):
        rows = [jnp.sum(x, axis=0, keepdims=True) for x in parts]
        part[i] = jnp.concatenate(rows + [jnp.zeros((T - len(rows), 128), F32)], axis=0)
        over_samp(lambda to: remote(part.at[i], red_s.at[i, s], rs_ss.at[i], rs_rs.at[i], (d, to)))
        red_s[i, s] = part[i]

    def pass_part(i):
        await_bytes(red_s.at[i, pl.ds(0, SAMP - 1)], rs_rs.at[i])
        red_d[i, d] = jnp.sum(red_s[i], axis=0)
        over_dom(lambda to: remote(red_d.at[i, d], red_d.at[i, d], rd_ss.at[i], rd_rs.at[i], (to, s)))

    def sums(i):
        await_bytes(red_d.at[i, pl.ds(0, DOM - 1)], rd_rs.at[i])
        total = jnp.sum(red_d[i], axis=0)
        return [jnp.sum(total[k : k + 1, :], axis=1, keepdims=True) for k in range(3)]

    zero = jnp.zeros((T, 128), F32)

    loads[0].wait()
    for j in range(2):
        for c in range(CH):
            rbuf[j, c, d] = jnp.zeros((2, T, 128), F32)
    widen(0, 0)
    over_dom(lambda to: pack(0, 0, to))
    pl.semaphore_wait(barrier, DOM + SAMP - 2)
    over_dom(lambda to: send_dom(0, 0, to))

    def early(c, _):
        widen(0, c)
        pack_and_send(0, c)
        return 0

    lax.fori_loop(1, CH, early, 0)

    def share_residual(c, _):
        forward(field.at[0], br, c, fr_ss, fr_rs)
        return 0

    lax.fori_loop(0, CH, share_residual, 0)

    loads[1].wait()

    def halves(row, _):
        high, low = split(w32[row])
        w16[row, :, 0:128] = high
        w16[row, :, 128:256] = low
        return 0

    lax.fori_loop(0, ROWS, halves, 0)
    for i in (2, 3, 4):
        loads[i].wait()

    def first(c, _):
        product(0, c)

        @pl.when(c > 0)
        def _():
            split_charge(0, c - 1)

        return 0

    lax.fori_loop(0, CH, first, 0)
    split_charge(0, CH - 1)

    def slopes(c, _):
        slo[chunk_of(c), :] = slope(c)
        over_samp(
            lambda to: remote(
                slo.at[place_of(c, to)], back.at[rows_of(c), slab_of(s)], back_ss, back_rs.at[c], (d, to)
            )
        )
        back[rows_of(c), slab_of(s)] = slo[place_of(c, s), :]
        return 0

    lax.fori_loop(0, CH, slopes, 0)

    def again(c, _):
        await_bytes(back.at[rows_of(c), pl.ds(0, N - SLAB)], back_rs.at[c])
        field[1, rows_of(c), :] = e[0, rows_of(c), :] + back[rows_of(c), :]
        widen(1, c)
        pack_and_send(1, c)
        return 0

    lax.fori_loop(0, CH, again, 0)

    def share_direct(c, _):
        forward(e.at[0], be.at[0], c, fe_ss.at[0], fe_rs.at[0])
        return 0

    lax.fori_loop(0, CH, share_direct, 0)

    def second(c, _):
        product(1, c)
        forward(e.at[1], be.at[1], c, fe_ss.at[1], fe_rs.at[1])

        @pl.when(c == 0)
        def _():
            await_bytes(br.at[pl.ds(0, ORDER - ORDER // SAMP)], fr_rs)
            await_bytes(be.at[0, pl.ds(0, ORDER - ORDER // SAMP)], fe_rs.at[0])

            def step(i, parts):
                one = slo[chunk_of(i), :] + be[0, chunk_of(i), :]
                z1b[chunk_of(i), :] = one
                start = br[chunk_of(i), :]
                return add_up(parts, (start * start, start * one, one * one))

            send_part(0, lax.fori_loop(0, CH, step, (zero, zero, zero)))

        @pl.when(c > 0)
        def _():
            split_charge(1, c - 1)

        @pl.when(c == 1)
        def _():
            pass_part(0)

        return 0

    lax.fori_loop(0, CH, second, 0)
    square, cross, image = sums(0)
    share = cross / square
    split_charge(1, CH - 1)
    await_bytes(be.at[1, pl.ds(0, ORDER - ORDER // SAMP)], fe_rs.at[1])

    def dots(c, parts):
        one = z1b[chunk_of(c), :]
        two = slope(c) + be[1, chunk_of(c), :] - share * one
        return add_up(parts, (br[chunk_of(c), :] * two, one * two, two * two))

    send_part(1, lax.fori_loop(0, CH, dots, (zero, zero, zero)))
    pass_part(1)

    for j in range(2):
        await_bytes(sbuf.at[j, :, pl.ds(0, DOM - 1)], dom_ss.at[j])
        await_bytes(q.at[j, :, pl.ds(0, N - SLAB)], fq_ss.at[j])
        await_bytes(e.at[j, :, pl.ds(0, N - SLAB)], fe_ss.at[j])
        await_bytes(red_s.at[j, pl.ds(0, SAMP - 1)], rs_ss.at[j])
    await_bytes(br.at[pl.ds(0, ORDER - ORDER // SAMP)], fr_ss)
    await_bytes(slo.at[pl.ds(0, ORDER - ORDER // SAMP)], back_ss)

    target, gram_cross, gram_second = sums(1)
    determinant = image * gram_second - gram_cross * gram_cross
    weight_first = (gram_second * cross - gram_cross * target) / determinant
    weight_second = (image * target - gram_cross * cross) / determinant

    def finish(c, _):
        residual = field[0, rows_of(c), :]
        out[rows_of(c), :] = weight_first * residual + weight_second * (field[1, rows_of(c), :] - share * residual)
        return 0

    lax.fori_loop(0, CH, finish, 0)
    for j in range(2):
        await_bytes(red_d.at[j, pl.ds(0, DOM - 1)], rd_ss.at[j])


def body(residual, conductance, capacitance, stamps, block_cols, send_blocks):
    smem = pl.BlockSpec(memory_space=pltpu.SMEM)
    anywhere = pl.BlockSpec(memory_space=pl.ANY)
    dma = pltpu.SemaphoreType.DMA
    here = (CH * T, N)
    all_samples = (ORDER, SLAB)
    vmem = pltpu.VMEM
    return pl.pallas_call(
        kernel,
        out_shape=jax.ShapeDtypeStruct(here, F32),
        in_specs=[smem, smem] + [anywhere] * 5,
        out_specs=pl.BlockSpec(memory_space=pltpu.VMEM),
        scratch_shapes=[
            vmem((2, *here), F32), vmem(here, F32), vmem(here, F32),
            vmem((ROWS, 256, 128), F32), vmem((ROWS, 256, 256), BF16),
            vmem((CH, 2 * CHUNK_ROWS, ORDER), BF16),
            vmem((ROWS, T, 128), F32), vmem((ROWS + SLOTS * DOM, 2 * T, 128), BF16),
            vmem((2, CH, DOM, 2, T, 128), F32), vmem((2, CH, DOM, 2, T, 128), F32),
            vmem((2, *here), F32), vmem((2, *here), F32),
            vmem((2, *all_samples), F32), vmem((2, *all_samples), F32), vmem(all_samples, F32),
            vmem(all_samples, BF16), vmem(all_samples, BF16), vmem(all_samples, F32), vmem(all_samples, F32), vmem(here, F32),
            vmem((2, T, 128), F32), vmem((2, SAMP, T, 128), F32), vmem((2, DOM, T, 128), F32),
            dma((5,)), dma((2,)), dma((2, CH)), dma((2,)), dma((2, CH)), dma((2,)), dma((2,)), dma, dma, dma, dma((CH,)),
            dma((2,)), dma((2,)), dma((2,)), dma((2,)),
        ],
        compiler_params=pltpu.CompilerParams(
            collective_id=0, has_side_effects=True, vmem_limit_bytes=56 * 2**20
        ),
        cost_estimate=pl.CostEstimate(flops=1_200_000_000, bytes_accessed=12_000_000, transcendentals=0),
        name="gmres_step",
    )(
        block_cols.T, send_blocks[0].T, residual, conductance, capacitance,
        stamps.reshape(ROWS, 256, 128), jnp.asarray(derivative_matrix()),
    )


def solution(mesh):
    in_specs = (
        P("samp", "dom"),
        P("samp", "dom"),
        P("samp", "dom"),
        P("dom", None, None, None),
        P("dom", None),
        P("dom", None, None),
    )
    return jax.shard_map(body, mesh=mesh, in_specs=in_specs, out_specs=P("samp", "dom"), check_vma=False)
```

time: 105 us -> 94.9 us (0.904)
  Pallas kernels: 99.9 us -> 92.9 us
  local copies, waits for them, and re-layouts: 4.77 us -> 1.87 us
    pallas_call x1, Pallas kernels: 99.9 us -> 92.9 us  [body(): pl.pallas_call(kernel, out_shape=jax.ShapeDtypeStruct(here, F32), in_spec...]
    unnamed x3 -> x1, local copies, waits for them, and re-layouts: 3.4 us -> 1.87 us
    reshape x2 -> x0, local copies, waits for them, and re-layouts: 1.37 us -> none  [the longest x1 0.7 us: body(): send_blocks.reshape(-1)]
where the time goes in v2:
time: 94.9 us; the launch traced here: 94.7 us
  Pallas kernels  92.9 us (98%)
  local copies, waits for them, and re-layouts  1.87 us (2%)
    pallas_call x1, Pallas kernels, body(): pl.pallas_call(kernel, out_shape=jax.ShapeDtypeStruct(here, F32), in_spec...  92.9 us

profile of v2, /device:TPU:1, one launch (start us, length us, event | category | flops | bytes accessed | tf_op | source)
XLA Modules:
  0.0 94.7 jit_solution(1825927079854562718)
XLA Ops:
  0.0 92.9 %gmres_step.1 = f32[32,4096]{1,0:T(8,128)} custom-call(s32[4,64]{1,0:T(4,128)} %bitcast.6, s32[4,32]{1,0:T(4,128)} %bitcast.7, f32[32,4096]{1,0:T(8,128)} %r_hbm.1, f32[32,4096]{1,0:T(8,128)} %cond_hbm.1, f32[32,4096]{1,0:T(8,128)} %cap_hbm.1, f32[64,256,128]{2,1,0:T(8,128)} %bitcast.5, bf16[4,128,256]{2,1,0:T(8,128)(2,1)} %constant.2.clone.dm_hbm), custom_call_target="tpu_custom_call" | custom-call | flops 1200000000 | bytes 12000000 | tf_op jit(solution)/shard_map/gmres_step/pallas_call | solution.py:374
  92.9 1.9 %copy.9 = f32[32,4096]{1,0:T(8,128)} copy(f32[32,4096]{1,0:T(8,128)} %gmres_step.1) | data formatting | bytes 1048576

commit v3 on v2

--- a/solution.py
+++ b/solution.py
@@ -19,6 +19,7 @@
 T = 8
 N = 4096
 SLAB = N // SAMP
+SQUARE = 16
 ORDER = 256
 CHUNK_ROWS = SAMP * T
 
@@ -44,11 +45,12 @@
 
 
 def kernel(
-    cols, send, r_hbm, cond_hbm, cap_hbm, w_hbm, dm_hbm, out,
+    cols_hbm, send_hbm, r_hbm, cond_hbm, cap_hbm, w_hbm, dm_hbm, out_hbm,
+    cols, send, out,
     field, cond, cap, w32, w16, dm, dup, ext,
     sbuf, rbuf, q, e, bq, be, br, bh, bl, z1b, slo, back, part, red_s, red_d,
     load_sem, dom_ss, dom_rs, fq_ss, fq_rs, fe_ss, fe_rs, fr_ss, fr_rs, back_ss, back_rs,
-    rs_ss, rs_rs, rd_ss, rd_rs,
+    rs_ss, rs_rs, rd_ss, rd_rs, out_sem,
 ):
     d = lax.axis_index("dom")
     s = lax.axis_index("samp")
@@ -58,7 +60,7 @@
     loads = [
         pltpu.make_async_copy(src, dst, load_sem.at[i])
         for i, (src, dst) in enumerate(
-            ((r_hbm, field.at[0]), (w_hbm, w32), (cond_hbm, cond), (cap_hbm, cap), (dm_hbm, dm))
+            ((r_hbm, field.at[0]), (send_hbm, send), (cols_hbm, cols), (w_hbm, w32), (cond_hbm, cond), (cap_hbm, cap), (dm_hbm, dm))
         )
     ]
     for copy in loads:
@@ -80,11 +82,40 @@
         for k in (4, 3, 5, 2, 6, 1, 7):
             act(lax.rem(s + k, SAMP))
 
+    z, y, x, core = lax.div(d, 4), lax.rem(d, 4), lax.div(s, 2), lax.rem(s, 2)
+
+    def over_square(act):
+        act(SQUARE // 2)
+
+        def step(m, _):
+            act(SQUARE // 2 + m)
+            act(SQUARE // 2 - m)
+            return 0
+
+        lax.fori_loop(1, SQUARE // 2, step, 0)
+
+    def in_plane(k):
+        return z * 4 + lax.rem(y + lax.rem(k, 4), 4), lax.rem(s + 2 * lax.div(k, 4), SAMP)
+
+    def in_line(k):
+        return lax.rem(d + 4 * lax.div(k, 2), DOM), 2 * x + lax.rem(core + lax.rem(k, 2), 2)
+
     def greet(to_dom, to_samp):
         pl.semaphore_signal(barrier, inc=1, device_id=(to_dom, to_samp), device_id_type=MESH)
 
     over_dom(lambda to: greet(to, s))
     over_samp(lambda to: greet(d, to))
+
+    def greet_rest(m, _):
+        greet(*in_plane(4 * (1 + lax.div(m, 3)) + 1 + lax.rem(m, 3)))
+        return 0
+
+    def greet_line(m, _):
+        greet(*in_line(2 * m + 1))
+        return 0
+
+    lax.fori_loop(0, 9, greet_rest, 0)
+    lax.fori_loop(1, 8, greet_line, 0)
 
     def remote(src, dst, send_sem, recv_sem, to):
         pltpu.make_async_remote_copy(
@@ -212,16 +243,18 @@
     def send_part(i, parts):
         rows = [jnp.sum(x, axis=0, keepdims=True) for x in parts]
         part[i] = jnp.concatenate(rows + [jnp.zeros((T - len(rows), 128), F32)], axis=0)
-        over_samp(lambda to: remote(part.at[i], red_s.at[i, s], rs_ss.at[i], rs_rs.at[i], (d, to)))
-        red_s[i, s] = part[i]
+        mine = x * 4 + y
+        over_square(lambda k: remote(part.at[i], red_s.at[i, mine], rs_ss.at[i], rs_rs.at[i], in_plane(k)))
+        red_s[i, mine] = part[i]
 
     def pass_part(i):
-        await_bytes(red_s.at[i, pl.ds(0, SAMP - 1)], rs_rs.at[i])
-        red_d[i, d] = jnp.sum(red_s[i], axis=0)
-        over_dom(lambda to: remote(red_d.at[i, d], red_d.at[i, d], rd_ss.at[i], rd_rs.at[i], (to, s)))
+        await_bytes(red_s.at[i, pl.ds(0, SQUARE - 1)], rs_rs.at[i])
+        mine = z * 2 + core
+        red_d[i, mine] = jnp.sum(red_s[i], axis=0)
+        over_square(lambda k: remote(red_d.at[i, mine], red_d.at[i, mine], rd_ss.at[i], rd_rs.at[i], in_line(k)))
 
     def sums(i):
-        await_bytes(red_d.at[i, pl.ds(0, DOM - 1)], rd_rs.at[i])
+        await_bytes(red_d.at[i, pl.ds(0, SQUARE - 1)], rd_rs.at[i])
         total = jnp.sum(red_d[i], axis=0)
         return [jnp.sum(total[k : k + 1, :], axis=1, keepdims=True) for k in range(3)]
 
@@ -232,8 +265,9 @@
         for c in range(CH):
             rbuf[j, c, d] = jnp.zeros((2, T, 128), F32)
     widen(0, 0)
+    loads[1].wait()
     over_dom(lambda to: pack(0, 0, to))
-    pl.semaphore_wait(barrier, DOM + SAMP - 2)
+    pl.semaphore_wait(barrier, DOM + SAMP - 2 + 9 + 7)
     over_dom(lambda to: send_dom(0, 0, to))
 
     def early(c, _):
@@ -249,7 +283,7 @@
 
     lax.fori_loop(0, CH, share_residual, 0)
 
-    loads[1].wait()
+    loads[3].wait()
 
     def halves(row, _):
         high, low = split(w32[row])
@@ -258,7 +292,7 @@
         return 0
 
     lax.fori_loop(0, ROWS, halves, 0)
-    for i in (2, 3, 4):
+    for i in (2, 4, 5, 6):
         loads[i].wait()
 
     def first(c, _):
@@ -331,11 +365,17 @@
     square, cross, image = sums(0)
     share = cross / square
     split_charge(1, CH - 1)
+
+    def last_slopes(c, _):
+        bq[0, chunk_of(c), :] = slope(c)
+        return 0
+
+    lax.fori_loop(0, CH, last_slopes, 0)
     await_bytes(be.at[1, pl.ds(0, ORDER - ORDER // SAMP)], fe_rs.at[1])
 
     def dots(c, parts):
         one = z1b[chunk_of(c), :]
-        two = slope(c) + be[1, chunk_of(c), :] - share * one
+        two = bq[0, chunk_of(c), :] + be[1, chunk_of(c), :] - share * one
         return add_up(parts, (br[chunk_of(c), :] * two, one * two, two * two))
 
     send_part(1, lax.fori_loop(0, CH, dots, (zero, zero, zero)))
@@ -345,7 +385,7 @@
         await_bytes(sbuf.at[j, :, pl.ds(0, DOM - 1)], dom_ss.at[j])
         await_bytes(q.at[j, :, pl.ds(0, N - SLAB)], fq_ss.at[j])
         await_bytes(e.at[j, :, pl.ds(0, N - SLAB)], fe_ss.at[j])
-        await_bytes(red_s.at[j, pl.ds(0, SAMP - 1)], rs_ss.at[j])
+        await_bytes(red_s.at[j, pl.ds(0, SQUARE - 1)], rs_ss.at[j])
     await_bytes(br.at[pl.ds(0, ORDER - ORDER // SAMP)], fr_ss)
     await_bytes(slo.at[pl.ds(0, ORDER - ORDER // SAMP)], back_ss)
 
@@ -357,15 +397,16 @@
     def finish(c, _):
         residual = field[0, rows_of(c), :]
         out[rows_of(c), :] = weight_first * residual + weight_second * (field[1, rows_of(c), :] - share * residual)
+        pltpu.make_async_copy(out.at[rows_of(c)], out_hbm.at[rows_of(c)], out_sem).start()
         return 0
 
     lax.fori_loop(0, CH, finish, 0)
     for j in range(2):
-        await_bytes(red_d.at[j, pl.ds(0, DOM - 1)], rd_ss.at[j])
+        await_bytes(red_d.at[j, pl.ds(0, SQUARE - 1)], rd_ss.at[j])
+    pltpu.make_async_copy(out, out_hbm, out_sem).wait()
 
 
 def body(residual, conductance, capacitance, stamps, block_cols, send_blocks):
-    smem = pl.BlockSpec(memory_space=pltpu.SMEM)
     anywhere = pl.BlockSpec(memory_space=pl.ANY)
     dma = pltpu.SemaphoreType.DMA
     here = (CH * T, N)
@@ -374,9 +415,10 @@
     return pl.pallas_call(
         kernel,
         out_shape=jax.ShapeDtypeStruct(here, F32),
-        in_specs=[smem, smem] + [anywhere] * 5,
-        out_specs=pl.BlockSpec(memory_space=pltpu.VMEM),
+        in_specs=[anywhere] * 7,
+        out_specs=anywhere,
         scratch_shapes=[
+            pltpu.SMEM((4, ROWS), jnp.int32), pltpu.SMEM((SLOTS, DOM), jnp.int32), vmem(here, F32),
             vmem((2, *here), F32), vmem(here, F32), vmem(here, F32),
             vmem((ROWS, 256, 128), F32), vmem((ROWS, 256, 256), BF16),
             vmem((CH, 2 * CHUNK_ROWS, ORDER), BF16),
@@ -385,9 +427,9 @@
             vmem((2, *here), F32), vmem((2, *here), F32),
             vmem((2, *all_samples), F32), vmem((2, *all_samples), F32), vmem(all_samples, F32),
             vmem(all_samples, BF16), vmem(all_samples, BF16), vmem(all_samples, F32), vmem(all_samples, F32), vmem(here, F32),
-            vmem((2, T, 128), F32), vmem((2, SAMP, T, 128), F32), vmem((2, DOM, T, 128), F32),
-            dma((5,)), dma((2,)), dma((2, CH)), dma((2,)), dma((2, CH)), dma((2,)), dma((2,)), dma, dma, dma, dma((CH,)),
-            dma((2,)), dma((2,)), dma((2,)), dma((2,)),
+            vmem((2, T, 128), F32), vmem((2, SQUARE, T, 128), F32), vmem((2, SQUARE, T, 128), F32),
+            dma((7,)), dma((2,)), dma((2, CH)), dma((2,)), dma((2, CH)), dma((2,)), dma((2,)), dma, dma, dma, dma((CH,)),
+            dma((2,)), dma((2,)), dma((2,)), dma((2,)), dma,
         ],
         compiler_params=pltpu.CompilerParams(
             collective_id=0, has_side_effects=True, vmem_limit_bytes=56 * 2**20

time: 94.9 us -> 93 us (0.980)
  Pallas kernels: 92.9 us -> 91 us
    pallas_call x1, Pallas kernels: 92.9 us -> 91 us  [body(): pl.pallas_call(kernel, out_shape=jax.ShapeDtypeStruct(here, F32), in_spec...]
where the time goes in v3:
time: 93 us; the launch traced here: 92.8 us
  Pallas kernels  91 us (98%)
  local copies, waits for them, and re-layouts  1.87 us (2%)
    pallas_call x1, Pallas kernels, body(): pl.pallas_call(kernel, out_shape=jax.ShapeDtypeStruct(here, F32), in_spec...  91 us
    unnamed x1, local copies, waits for them, and re-layouts  1.87 us

profile of v3, /device:TPU:1, one launch (start us, length us, event | category | flops | bytes accessed | tf_op | source)
XLA Modules:
  0.0 92.8 jit_solution(155283653425103980)
XLA Ops:
  0.0 91.0 %gmres_step.1 = f32[32,4096]{1,0:T(8,128)} custom-call(s32[4,64]{1,0:T(4,128)} %bitcast.6, s32[4,32]{1,0:T(4,128)} %bitcast.7, f32[32,4096]{1,0:T(8,128)} %r_hbm.1, f32[32,4096]{1,0:T(8,128)} %cond_hbm.1, f32[32,4096]{1,0:T(8,128)} %cap_hbm.1, f32[64,256,128]{2,1,0:T(8,128)} %bitcast.5, bf16[4,128,256]{2,1,0:T(8,128)(2,1)} %constant.2.clone.dm_hbm), custom_call_target="tpu_custom_call" | custom-call | flops 1200000000 | bytes 12000000 | tf_op jit(solution)/shard_map/gmres_step/pallas_call | solution.py:415
  91.0 1.9 %copy.9 = f32[32,4096]{1,0:T(8,128)} copy(f32[32,4096]{1,0:T(8,128)} %gmres_step.1) | data formatting | bytes 1048576

commit v4 on v3

--- a/solution.py
+++ b/solution.py
@@ -76,7 +76,7 @@
             act(lax.rem(d + DOM // 2 - m, DOM))
             return 0
 
-        lax.fori_loop(1, DOM // 2, step, 0)
+        lax.fori_loop(1, DOM // 2, step, 0, unroll=3)
 
     def over_samp(act):
         for k in (4, 3, 5, 2, 6, 1, 7):
@@ -181,7 +181,7 @@
             spread(field[j, rows_of(c), tile_of(p)], 2 * p)
             return 0
 
-        lax.fori_loop(0, ROWS // 2, local, 0, unroll=16)
+        lax.fori_loop(0, ROWS // 2, local, 0, unroll=32)
         await_bytes(rbuf.at[j, c, pl.ds(0, DOM - 1)], dom_rs.at[j, c])
 
         def arrived(k, _):
@@ -189,7 +189,7 @@
                 spread(rbuf[j, c, k, h], ROWS + SLOTS * k + 2 * h)
             return 0
 
-        lax.fori_loop(0, DOM, arrived, 0, unroll=8)
+        lax.fori_loop(0, DOM, arrived, 0, unroll=16)
 
         def one_row(row):
             picked = [ext[cols[k, row]] for k in range(4)]
@@ -291,7 +291,7 @@
         w16[row, :, 128:256] = low
         return 0
 
-    lax.fori_loop(0, ROWS, halves, 0)
+    lax.fori_loop(0, ROWS, halves, 0, unroll=2)
     for i in (2, 4, 5, 6):
         loads[i].wait()
 
@@ -370,7 +370,7 @@
         bq[0, chunk_of(c), :] = slope(c)
         return 0
 
-    lax.fori_loop(0, CH, last_slopes, 0)
+    lax.fori_loop(0, CH, last_slopes, 0, unroll=4)
     await_bytes(be.at[1, pl.ds(0, ORDER - ORDER // SAMP)], fe_rs.at[1])
 
     def dots(c, parts):
@@ -378,7 +378,7 @@
         two = bq[0, chunk_of(c), :] + be[1, chunk_of(c), :] - share * one
         return add_up(parts, (br[chunk_of(c), :] * two, one * two, two * two))
 
-    send_part(1, lax.fori_loop(0, CH, dots, (zero, zero, zero)))
+    send_part(1, lax.fori_loop(0, CH, dots, (zero, zero, zero), unroll=4))
     pass_part(1)
 
     for j in range(2):

time: 93 us -> 92.5 us (level)
  no operation moved by 1% of the time
where the time goes in v4:
time: 92.5 us; the launch traced here: 92.4 us
  Pallas kernels  90.5 us (98%)
  local copies, waits for them, and re-layouts  1.87 us (2%)
    pallas_call x1, Pallas kernels, body(): pl.pallas_call(kernel, out_shape=jax.ShapeDtypeStruct(here, F32), in_spec...  90.5 us
    unnamed x1, local copies, waits for them, and re-layouts  1.87 us

profile of v4, /device:TPU:1, one launch (start us, length us, event | category | flops | bytes accessed | tf_op | source)
XLA Modules:
  0.0 92.4 jit_solution(3310646735123047176)
XLA Ops:
  0.0 90.5 %gmres_step.1 = f32[32,4096]{1,0:T(8,128)} custom-call(s32[4,64]{1,0:T(4,128)} %bitcast.6, s32[4,32]{1,0:T(4,128)} %bitcast.7, f32[32,4096]{1,0:T(8,128)} %r_hbm.1, f32[32,4096]{1,0:T(8,128)} %cond_hbm.1, f32[32,4096]{1,0:T(8,128)} %cap_hbm.1, f32[64,256,128]{2,1,0:T(8,128)} %bitcast.5, bf16[4,128,256]{2,1,0:T(8,128)(2,1)} %constant.2.clone.dm_hbm), custom_call_target="tpu_custom_call" | custom-call | flops 1200000000 | bytes 12000000 | tf_op jit(solution)/shard_map/gmres_step/pallas_call | solution.py:415
  90.6 1.9 %copy.9 = f32[32,4096]{1,0:T(8,128)} copy(f32[32,4096]{1,0:T(8,128)} %gmres_step.1) | data formatting | bytes 1048576

commit v5 on v4

--- a/solution.py
+++ b/solution.py
@@ -355,7 +355,7 @@
         def _():
             split_charge(1, c - 1)
 
-        @pl.when(c == 1)
+        @pl.when(c == 2)
         def _():
             pass_part(0)
 

time: 92.5 us -> 92.3 us (level)
  no operation moved by 1% of the time
where the time goes in v5:
time: 92.3 us; the launch traced here: 92.2 us
  Pallas kernels  90.3 us (98%)
  local copies, waits for them, and re-layouts  1.87 us (2%)
    pallas_call x1, Pallas kernels, body(): pl.pallas_call(kernel, out_shape=jax.ShapeDtypeStruct(here, F32), in_spec...  90.3 us
    unnamed x1, local copies, waits for them, and re-layouts  1.87 us

profile of v5, /device:TPU:1, one launch (start us, length us, event | category | flops | bytes accessed | tf_op | source)
XLA Modules:
  0.0 92.2 jit_solution(10886942964237953939)
XLA Ops:
  0.0 90.3 %gmres_step.1 = f32[32,4096]{1,0:T(8,128)} custom-call(s32[4,64]{1,0:T(4,128)} %bitcast.6, s32[4,32]{1,0:T(4,128)} %bitcast.7, f32[32,4096]{1,0:T(8,128)} %r_hbm.1, f32[32,4096]{1,0:T(8,128)} %cond_hbm.1, f32[32,4096]{1,0:T(8,128)} %cap_hbm.1, f32[64,256,128]{2,1,0:T(8,128)} %bitcast.5, bf16[4,128,256]{2,1,0:T(8,128)(2,1)} %constant.2.clone.dm_hbm), custom_call_target="tpu_custom_call" | custom-call | flops 1200000000 | bytes 12000000 | tf_op jit(solution)/shard_map/gmres_step/pallas_call | solution.py:415
  90.3 1.9 %copy.9 = f32[32,4096]{1,0:T(8,128)} copy(f32[32,4096]{1,0:T(8,128)} %gmres_step.1) | data formatting | bytes 1048576
